TPU v7x, 32 devices: a whole 2x2x4 slice. The times are simulated.
32 devices in a mesh: dp: 4 (over x, core), expert: 8 (over z, y).
Axes of the slice: x: 2, y: 2, z: 4, core: 2. Of those that a mesh axis runs over, the one named last changes fastest.
Arguments:
- tokens: bfloat16 [1024, 3584], P(('dp', 'expert')), may hold values from -6 to 6
- expert_ids: int32 [1024, 2], P(('dp', 'expert')), may hold values from 0 to 7, all different within a row; in each aligned block of 32 rows (0 to 31, 32 to 63, ...) at most 12 rows name the same one
- mix_weights: float32 [1024, 2], P(('dp', 'expert')), may hold values from 0.25 to 1
- w_up: bfloat16 [8, 3584, 3072], P('expert', None, 'dp'), may hold values from -0.09375 to 0.09375
- w_down: bfloat16 [8, 3072, 3584], P('expert', 'dp'), may hold values from -0.109375 to 0.109375
- out_grad: bfloat16 [1024, 3584], P(('dp', 'expert')), may hold values from -3 to 3
Outputs:
- layer_out: bfloat16 [1024, 3584], P(('dp', 'expert'))
- token_grad: bfloat16 [1024, 3584], P(('dp', 'expert'))
- up_grad: bfloat16 [8, 3584, 3072], P('expert', None, 'dp')
- down_grad: bfloat16 [8, 3072, 3584], P('expert', 'dp')
Inputs may be any that keep to these rules, and one draw needn't show every extreme that they name: `expert_ids`: the two experts of a token differ. The 32 tokens of one device name one expert at most 12 times, and in every draw some device names some expert exactly 12 times.
All inputs are finite; a program needn't handle non-finite values.
Results may differ from a plain program's by a relative error of at most 0.015.
Values may be sent and summed in bfloat16 or wider, within the bound.
A program may use at most 128 MiB of HBM per device.

v0:
```python
import jax
import jax.numpy as jnp
from jax import lax
from jax.sharding import PartitionSpec as P


def spread(token_send, grad_send):
    token_moved, grad_moved = (
        lax.all_to_all(token_send, "expert", split_axis=0, concat_axis=0, tiled=True),
        lax.all_to_all(grad_send, "expert", split_axis=0, concat_axis=0, tiled=True),
    )
    return (
        lax.all_gather(token_moved, "dp", axis=0, tiled=True),
        lax.all_gather(grad_moved, "dp", axis=0, tiled=True),
    )


def per_device(tokens, expert_ids, mix_weights, w_up, w_down, out_grad):
    tok_count = tokens.shape[0]
    owner_count = lax.axis_size("expert")
    expert_count = owner_count * w_up.shape[0]
    capacity = max(2, 3 * tok_count // expert_count)
    slot_count = expert_count * capacity
    one_hot = (
        expert_ids[:, :, None] == jnp.arange(expert_count, dtype=jnp.int32)[None, None, :]
    ).astype(jnp.int32)
    pair_hits = one_hot.reshape(tok_count * 2, expert_count)
    before = jnp.cumsum(pair_hits, axis=0) - pair_hits
    position = jnp.sum(before * pair_hits, axis=1)
    target = expert_ids.reshape(-1) * capacity + position
    placing = (target[:, None] == jnp.arange(slot_count, dtype=jnp.int32)[None, :]).reshape(
        tok_count, 2, slot_count
    )
    select = jnp.sum(placing.astype(jnp.bfloat16), axis=1)
    weighting = jnp.sum(placing.astype(jnp.float32) * mix_weights[:, :, None], axis=1)
    token_send = lax.dot_general(
        select, tokens, (((0,), (0,)), ((), ())), preferred_element_type=jnp.float32
    ).astype(jnp.bfloat16)
    grad_send = lax.dot_general(
        weighting,
        out_grad.astype(jnp.float32),
        (((0,), (0,)), ((), ())),
        precision=lax.Precision.HIGHEST,
    ).astype(jnp.bfloat16)
    token_rows, grad_rows = spread(token_send, grad_send)
    up_local = w_up[0]
    down_local = w_down[0]
    pre_act = jnp.dot(token_rows, up_local, preferred_element_type=jnp.float32)
    squash = jax.nn.sigmoid(pre_act)
    hidden = (pre_act * squash).astype(jnp.bfloat16)
    piece = hidden
    term = jnp.dot(piece, down_local, preferred_element_type=jnp.float32)
    out_rows = lax.psum_scatter(
        lax.optimization_barrier(term.astype(jnp.bfloat16))
        .astype(jnp.float32)
        .astype(jnp.bfloat16),
        "dp",
        scatter_dimension=0,
        tiled=True,
    )
    hidden_grad = lax.dot_general(
        grad_rows, down_local, (((1,), (1,)), ((), ())), preferred_element_type=jnp.float32
    )
    grad_down = lax.dot_general(
        hidden, grad_rows, (((0,), (0,)), ((), ())), preferred_element_type=jnp.float32
    )
    slope = squash * (1.0 + pre_act * (1.0 - squash))
    pre_grad = (hidden_grad * slope).astype(jnp.bfloat16)
    grad_up = lax.dot_general(
        token_rows, pre_grad, (((0,), (0,)), ((), ())), preferred_element_type=jnp.float32
    )
    piece = pre_grad
    term = lax.dot_general(
        piece, up_local, (((1,), (1,)), ((), ())), preferred_element_type=jnp.float32
    )
    in_rows = lax.psum_scatter(
        lax.optimization_barrier(term.astype(jnp.bfloat16))
        .astype(jnp.float32)
        .astype(jnp.bfloat16),
        "dp",
        scatter_dimension=0,
        tiled=True,
    )
    out_back = lax.all_to_all(out_rows, "expert", split_axis=0, concat_axis=0, tiled=True)
    in_back = lax.all_to_all(in_rows, "expert", split_axis=0, concat_axis=0, tiled=True)
    layer_out = lax.dot_general(
        weighting,
        out_back.astype(jnp.float32),
        (((1,), (0,)), ((), ())),
        precision=lax.Precision.HIGHEST,
    ).astype(jnp.bfloat16)
    token_grad = lax.dot_general(
        select, in_back, (((1,), (0,)), ((), ())), preferred_element_type=jnp.float32
    ).astype(jnp.bfloat16)
    return (
        layer_out,
        token_grad,
        grad_up.astype(jnp.bfloat16)[None],
        grad_down.astype(jnp.bfloat16)[None],
    )


def solution(mesh):
    in_specs = (
        P(("dp", "expert"), None),
        P(("dp", "expert"), None),
        P(("dp", "expert"), None),
        P("expert", None, "dp"),
        P("expert", "dp", None),
        P(("dp", "expert"), None),
    )
    out_specs = (
        P(("dp", "expert"), None),
        P(("dp", "expert"), None),
        P("expert", None, "dp"),
        P("expert", "dp", None),
    )
    return jax.shard_map(
        per_device, mesh=mesh, in_specs=in_specs, out_specs=out_specs, check_vma=False
    )
```

profile of v0, /device:TPU:28, one launch (start us, length us, event | category | flops | bytes accessed | tf_op | source)
XLA Modules:
  0.0 206.9 jit_solution(15873166865207856767)
XLA Ops:
  7.2 0.8 copy.22
  8.7 0.7 multiply_add_fusion
  10.0 26.4 %all_to_all.48 = bf16[8,12,3584]{2,1,0:T(8,128)(2,1)S(1)} all-to-all(bf16[8,12,3584]{2,1,0:T(8,128)(2,1)S(1)} %all_to_all.32), channel_id=1, replica_groups=mesh['dp'=4,'expert'=8] {'expert'}, dimensions={0} | all-to-all | bytes 1376256 | tf_op jit(solution)/shard_map/all_to_all | solution.py:9
  36.4 1.0 all_to_all.34
  37.6 0.7 convolution_convert_fusion.4
  38.5 26.2 %all_to_all.49 = bf16[8,12,3584]{2,1,0:T(8,128)(2,1)S(1)} all-to-all(bf16[8,12,3584]{2,1,0:T(8,128)(2,1)S(1)} %all_to_all.38), channel_id=1, replica_groups=mesh['dp'=4,'expert'=8] {'expert'}, dimensions={0} | all-to-all | bytes 1376256 | tf_op jit(solution)/shard_map/all_to_all | solution.py:10
  64.6 1.0 all_to_all.40
  65.8 5.7 %fusion.6 = f32[384,768]{1,0:T(8,128)S(1)} fusion(bf16[384,3584]{1,0:T(8,128)(2,1)} %all-gather.3.cloned.1.call-done, bf16[1,3584,768]{2,1,0:T(8,128)(2,1)} %param.9), kind=kOutput, calls=%fused_computation.10 | convolution fusion | flops 2113929216 | bytes 9437184 | tf_op jit(solution)/shard_map/dot_general | solution.py:48
  71.4 6.6 %convolution_convert_fusion.3 = bf16[384,3584]{1,0:T(8,128)(2,1)} fusion(bf16[1,768,3584]{2,1,0:T(8,128)(2,1)} %param.10, f32[384,768]{1,0:T(8,128)S(1)} %fusion.6), kind=kOutput, calls=%fused_computation.5 | convolution fusion | flops 2116780032 | bytes 9437184 | tf_op jit(solution)/shard_map/dot_general | solution.py:52
  78.2 15.1 %all-gather.5.cloned.1.call-done = bf16[384,3584]{1,0:T(8,128)(2,1)} async-done(((bf16[96,3584]{1,0:T(8,128)(2,1)}), bf16[384,3584]{1,0:T(8,128)(2,1)}) %all-gather.5.cloned.1.call-update) | async-done | bytes 2752528 | tf_op jit(solution)/shard_map/all_gather | solution.py:14
  93.3 5.8 %fusion.11 = bf16[384,768]{1,0:T(8,128)(2,1)S(1)} fusion(bf16[384,3584]{1,0:T(8,128)(2,1)} %all-gather.5.cloned.1.call-done, bf16[1,768,3584]{2,1,0:T(8,128)(2,1)} %param.10, f32[384,768]{1,0:T(8,128)S(1)} %fusion.6), kind=kOutput, calls=%fused_computation.17 | convolution fusion | flops 2116583424 | bytes 10027008 | tf_op jit(solution)/shard_map/dot_general | solution.py:61
  99.1 0.8 copy-done.4
  99.9 6.8 %convolution_convert_fusion.2 = bf16[384,3584]{1,0:T(8,128)(2,1)} fusion(bf16[384,768]{1,0:T(8,128)(2,1)S(1)} %fusion.11, bf16[1,3584,768]{2,1,0:T(8,128)(2,1)} %param.9), kind=kOutput, calls=%fused_computation.4 | convolution fusion | flops 2115305472 | bytes 8847360 | tf_op jit(solution)/shard_map/dot_general | solution.py:73
  106.7 25.2 %reduce-scatter.3.cloned.1.call-done = bf16[96,3584]{1,0:T(8,128)(2,1)} async-done(((bf16[384,3584]{1,0:T(8,128)(2,1)}), bf16[96,3584]{1,0:T(8,128)(2,1)}) %reduce-scatter.3.cloned.1.call-update) | async-done | bytes 688144 | tf_op jit(solution)/shard_map/reduce_scatter | solution.py:53
  131.9 2.1 %all_to_all.35 = bf16[8,12,3584]{2,1,0:T(8,128)(2,1)} reshape(bf16[96,3584]{1,0:T(8,128)(2,1)} %reduce-scatter.3.cloned.1.call-done) | data formatting | bytes 1376256 | tf_op jit(solution)/shard_map/all_to_all | solution.py:84
  134.0 6.0 %all-to-all-start.1 = ((bf16[8,12,3584]{2,1,0:T(8,128)(2,1)}), bf16[8,12,3584]{2,1,0:T(8,128)(2,1)S(1)}, u32[]{:S(2)}, u32[]{:S(2)}) async-start(bf16[8,12,3584]{2,1,0:T(8,128)(2,1)} %all_to_all.35), calls=%async_computation.2 | async-start | bytes 1835008 | tf_op jit(solution)/shard_map/all_to_all | solution.py:84
  140.0 30.6 %reduce-scatter.5.cloned.1.call-done = bf16[96,3584]{1,0:T(8,128)(2,1)} async-done(((bf16[384,3584]{1,0:T(8,128)(2,1)}), bf16[96,3584]{1,0:T(8,128)(2,1)}) %reduce-scatter.5.cloned.1.call-update) | async-done | bytes 688144 | tf_op jit(solution)/shard_map/reduce_scatter | solution.py:76
  170.6 2.1 %all_to_all.41 = bf16[8,12,3584]{2,1,0:T(8,128)(2,1)} reshape(bf16[96,3584]{1,0:T(8,128)(2,1)} %reduce-scatter.5.cloned.1.call-done) | data formatting | bytes 1376256 | tf_op jit(solution)/shard_map/all_to_all | solution.py:85
  172.7 6.0 %all-to-all-start.3 = ((bf16[8,12,3584]{2,1,0:T(8,128)(2,1)}), bf16[8,12,3584]{2,1,0:T(8,128)(2,1)S(1)}, u32[]{:S(2)}, u32[]{:S(2)}) async-start(bf16[8,12,3584]{2,1,0:T(8,128)(2,1)} %all_to_all.41), calls=%async_computation.5 | async-start | bytes 1835008 | tf_op jit(solution)/shard_map/all_to_all | solution.py:85
  178.7 7.5 %fusion = bf16[1,3584,768]{2,1,0:T(8,128)(2,1)} fusion(bf16[384,3584]{1,0:T(8,128)(2,1)} %all-gather.3.cloned.1.call-done, bf16[384,768]{1,0:T(8,128)(2,1)} %copy-done.4), kind=kOutput, calls=%fused_computation.2 | convolution fusion | flops 2116681728 | bytes 8847360 | tf_op jit(solution)/shard_map/dot_general | solution.py:69
  186.2 4.9 %fusion.1 = bf16[1,768,3584]{2,1,0:T(8,128)(2,1)} fusion(bf16[384,3584]{1,0:T(8,128)(2,1)S(1)} %copy-done.3, f32[384,768]{1,0:T(8,128)S(1)} %fusion.6), kind=kOutput, calls=%fused_computation.3 | convolution fusion | flops 2118156288 | bytes 9437184 | tf_op jit(solution)/shard_map/dot_general | solution.py:64
  191.3 1.1 convolution_convert_fusion.7
  192.4 6.9 %all-to-all-done.3 = bf16[8,12,3584]{2,1,0:T(8,128)(2,1)S(1)} async-done(((bf16[8,12,3584]{2,1,0:T(8,128)(2,1)}), bf16[8,12,3584]{2,1,0:T(8,128)(2,1)S(1)}, u32[]{:S(2)}, u32[]{:S(2)}) %all-to-all-start.3) | async-done | bytes 688160 | tf_op jit(solution)/shard_map/all_to_all | solution.py:85
  199.4 0.9 convolution_convert_fusion.6
  (32 shorter events, 2.1 us)
Async XLA Ops:
  7.2 2.3 %copy-start = (bf16[32,3584]{1,0:T(8,128)(2,1)S(1)}, bf16[32,3584]{1,0:T(8,128)(2,1)}, u32[]{:S(2)}) copy-start(bf16[32,3584]{1,0:T(8,128)(2,1)} %param.6) | copy-start | bytes 688132
  7.2 58.6 %all-gather.3.cloned.1.call-start = ((), (), s32[]{:S(2)}) async-start(), calls=%async_computation.6 | async-start | bytes 3440640 | tf_op jit(solution)/shard_map/all_gather | solution.py:13
  9.8 27.6 %copy-start.2 = (f32[32,2]{0,1:T(2,128)S(1)}, f32[32,2]{0,1:T(2,128)}, u32[]{:S(2)}) copy-start(f32[32,2]{0,1:T(2,128)} %param.8) | copy-start | bytes 772
  9.9 27.7 %copy-start.1 = (bf16[32,3584]{1,0:T(8,128)(2,1)S(1)}, bf16[32,3584]{1,0:T(8,128)(2,1)}, u32[]{:S(2)}) copy-start(bf16[32,3584]{1,0:T(8,128)(2,1)} %param.11) | copy-start | bytes 688132
  37.4 55.8 %all-gather.5.cloned.1.call-start = ((), (), s32[]{:S(2)}) async-start(), calls=%async_computation.8 | async-start | bytes 3440640 | tf_op jit(solution)/shard_map/all_gather | solution.py:14
  65.7 66.2 %reduce-scatter.3.cloned.1.call-start = ((), (), s32[]{:S(2)}) async-start(), calls=%async_computation.7 | async-start | bytes 3440640 | tf_op jit(solution)/shard_map/reduce_scatter | solution.py:53
  78.1 92.5 %reduce-scatter.5.cloned.1.call-start = ((), (), s32[]{:S(2)}) async-start(), calls=%async_computation.9 | async-start | bytes 3440640 | tf_op jit(solution)/shard_map/reduce_scatter | solution.py:76
  99.1 0.8 copy-start.4
  134.0 38.7 %all-to-all-start.1 = ((bf16[8,12,3584]{2,1,0:T(8,128)(2,1)}), bf16[8,12,3584]{2,1,0:T(8,128)(2,1)S(1)}, u32[]{:S(2)}, u32[]{:S(2)}) async-start(bf16[8,12,3584]{2,1,0:T(8,128)(2,1)} %all_to_all.35), calls=%async_computation.2 | async-start | bytes 1835008 | tf_op jit(solution)/shard_map/all_to_all | solution.py:84
  172.7 26.6 %all-to-all-start.3 = ((bf16[8,12,3584]{2,1,0:T(8,128)(2,1)}), bf16[8,12,3584]{2,1,0:T(8,128)(2,1)S(1)}, u32[]{:S(2)}, u32[]{:S(2)}) async-start(bf16[8,12,3584]{2,1,0:T(8,128)(2,1)} %all_to_all.41), calls=%async_computation.5 | async-start | bytes 1835008 | tf_op jit(solution)/shard_map/all_to_all | solution.py:85
  178.7 7.6 %copy-start.3 = (bf16[384,3584]{1,0:T(8,128)(2,1)S(1)}, bf16[384,3584]{1,0:T(8,128)(2,1)}, u32[]{:S(2)}) copy-start(bf16[384,3584]{1,0:T(8,128)(2,1)} %all-gather.5.cloned.1.call-done) | copy-start | bytes 8257540
Sparse Core Ops, SparseCore 0:
  37.5 27.2 all-gather.2
  66.9 26.2 all-gather.4
  96.4 35.4 reduce-scatter.2
  135.1 35.4 reduce-scatter.4
where the time goes:
time: 211 us; the launch traced here: 207 us
  waiting for transfers between devices  77.8 us (37%)
  blocking collectives  52.5 us (25%)
  matrix products  40.5 us (19%)
  between operations  13.9 us (7%)
  starting transfers between devices  12.2 us (6%)
  local copies, waits for them, and re-layouts  8.75 us (4%)
    reduce_scatter x2, waiting for transfers between devices, per_device(): lax.psum_scatter(lax.optimization_barrier(term.astype(jnp.bfloat16)).asty...  55.8 us
    all_to_all x1, blocking collectives, spread(): lax.all_to_all(token_send, 'expert', split_axis=0, concat_axis=0, tiled=T...  26.4 us
    all_to_all x1, blocking collectives, spread(): lax.all_to_all(grad_send, 'expert', split_axis=0, concat_axis=0, tiled=True)  26.2 us
    all_gather x1, waiting for transfers between devices, spread(): lax.all_gather(grad_moved, 'dp', axis=0, tiled=True)  15.1 us
    dot_general x1, matrix products, per_device(): lax.dot_general(token_rows, pre_grad, (((0,), (0,)), ((), ())), preferred...  7.55 us
    all_to_all x1, waiting for transfers between devices, per_device(): lax.all_to_all(in_rows, 'expert', split_axis=0, concat_axis=0, tiled=True)  6.87 us
    dot_general x1, matrix products, per_device(): lax.dot_general(piece, up_local, (((1,), (1,)), ((), ())), preferred_elem...  6.76 us
    dot_general x1, matrix products, per_device(): term = jnp.dot(piece, down_local, preferred_element_type=jnp.float32)  6.64 us
  transfers between devices with their start and end apart: 6, of which 4 were waited for; matrix products, arithmetic and copies ran while one was open for 19% of the time, Pallas kernels for 0%

commit v1 on v0

v1 whole, which is shorter than its diff:
```python
import functools

import jax
import jax.numpy as jnp
import numpy as np
from jax import lax
from jax.experimental import pallas as pl
from jax.experimental.pallas import tpu as pltpu
from jax.sharding import PartitionSpec as P

MESH = pl.DeviceIdType.MESH
F32 = jnp.float32
BF16 = jnp.bfloat16
CHUNKS = 4


def contract(a, b, da, db):
    return lax.dot_general(a, b, (((da,), (db,)), ((), ())), preferred_element_type=F32)


def kernel(
    n_dp, n_ex, cap,
    ids_ref, mix_ref, tok_ref, og_ref, perm_ref, perm_t_ref, up_hbm, down_hbm,
    lay_ref, tg_ref, up_out, down_out,
    place, up_v, down_v, send, gath, part, pre_act, hidden, pre_grad,
    pair_in, cross_in, back_in,
    w_sem, a_snd, a_rcv, x_snd, x_rcv, p_snd, p_rcv,
    c_snd, c_rcv, r_snd, r_rcv, b_snd, b_rcv, out_sem,
):
    toks = tok_ref.shape[0]
    chunk = gath.shape[-1]
    block = CHUNKS * cap
    slots = n_ex * block
    group = n_ex * cap
    n_x = n_dp // 2
    dp = lax.axis_index("dp")
    ex = lax.axis_index("expert")
    x = dp // 2
    core = dp % 2
    mate = 2 * x + (1 - core)

    def xpeer(o):
        return 2 * ((x + o) % n_x) + core

    def xsource(o):
        return (x + n_x - o) % n_x

    barrier = pltpu.get_barrier_semaphore()
    for o in range(1, n_ex):
        pl.semaphore_signal(barrier, inc=1, device_id=(dp, (ex + o) % n_ex), device_id_type=MESH)
    for o in range(1, n_x):
        pl.semaphore_signal(barrier, inc=1, device_id=(xpeer(o), ex), device_id_type=MESH)
    pl.semaphore_signal(barrier, inc=1, device_id=(mate, ex), device_id_type=MESH)

    up_load = pltpu.make_async_copy(up_hbm, up_v, w_sem.at[0])
    down_load = pltpu.make_async_copy(down_hbm, down_v, w_sem.at[1])
    up_load.start()
    down_load.start()

    lower = (
        lax.broadcasted_iota(jnp.int32, (toks, toks), 1)
        < lax.broadcasted_iota(jnp.int32, (toks, toks), 0)
    )
    lower = jnp.where(lower, 1.0, 0.0).astype(BF16)
    lane = lax.broadcasted_iota(jnp.int32, (toks, n_ex), 1)
    id0, id1 = ids_ref[:, 0:1], ids_ref[:, 1:2]
    hit0 = jnp.where(lane == id0, 1.0, 0.0)
    hit1 = jnp.where(lane == id1, 1.0, 0.0)
    before0 = jnp.dot(lower, hit0.astype(BF16), preferred_element_type=F32)
    before1 = jnp.dot(lower, hit1.astype(BF16), preferred_element_type=F32) + jnp.sum(
        hit0, axis=0, keepdims=True
    )
    pos0 = jnp.sum(before0 * hit0, axis=1, keepdims=True).astype(jnp.int32)
    pos1 = jnp.sum(before1 * hit1, axis=1, keepdims=True).astype(jnp.int32)
    slot = lax.broadcasted_iota(jnp.int32, (toks, slots), 1)
    for k, (ids, pos) in enumerate(((id0, pos0), (id1, pos1))):
        for c in range(CHUNKS):
            hit = slot == ids * block + pos + c * cap
            place[k, c * toks:(c + 1) * toks, :] = jnp.where(hit, 1.0, 0.0).astype(BF16)

    def rows_of(e):
        return pl.ds(pl.multiple_of(e * block, 16), block)

    def stacked(value):
        return jnp.concatenate(
            [value[:, c * chunk:(c + 1) * chunk] for c in range(CHUNKS)], axis=0
        )

    def a2a(s, o, to):
        src = (ex + o) % n_ex
        return pltpu.make_async_remote_copy(
            src_ref=send.at[s, rows_of(src)],
            dst_ref=gath.at[s, dp, rows_of(to)],
            send_sem=a_snd.at[s, o], recv_sem=a_rcv.at[s, o],
            device_id=(dp, src), device_id_type=MESH,
        )

    def forward_x(s, ox, o):
        src = (ex + n_ex - o) % n_ex
        return pltpu.make_async_remote_copy(
            src_ref=gath.at[s, dp, rows_of(src)],
            dst_ref=gath.at[s, dp, rows_of(src)],
            send_sem=x_snd.at[s, ox, o], recv_sem=x_rcv.at[s, ox, o],
            device_id=(xpeer(ox), ex), device_id_type=MESH,
        )

    def arrived_x(s, ox, o):
        src = (ex + n_ex - o) % n_ex
        owner = 2 * xsource(ox) + core
        return pltpu.make_async_remote_copy(
            src_ref=gath.at[s, owner, rows_of(src)],
            dst_ref=gath.at[s, owner, rows_of(src)],
            send_sem=x_snd.at[s, ox, o], recv_sem=x_rcv.at[s, ox, o],
            device_id=(xpeer(ox), ex), device_id_type=MESH,
        )

    def mate_copy(s, ox, o, half):
        src = (ex + n_ex - o) % n_ex
        owner = 2 * xsource(ox) + half
        return pltpu.make_async_remote_copy(
            src_ref=gath.at[s, owner, rows_of(src)],
            dst_ref=gath.at[s, owner, rows_of(src)],
            send_sem=p_snd.at[s, ox, o], recv_sem=p_rcv.at[s, ox, o],
            device_id=(mate, ex), device_id_type=MESH,
        )

    def launch(s):
        gath[s, dp, rows_of(ex), :] = send[s, rows_of(ex), :]

        @pl.loop(1, n_ex)
        def _(o):
            a2a(s, o, ex).start()

    def spread_own(s, o):
        for ox in range(1, n_x):
            forward_x(s, ox, o).start()
        mate_copy(s, 0, o, core).start()

    def spread_cross(s, o):
        for ox in range(1, n_x):
            arrived_x(s, ox, o).wait_recv()
            mate_copy(s, ox, o, core).start()

    def own_arrival(s, o):
        a2a(s, o, (ex + n_ex - o) % n_ex).wait_recv()
        spread_own(s, o)

    def gathered(s):
        @pl.loop(0, n_ex)
        def _(o):
            for ox in range(n_x):
                mate_copy(s, ox, o, 1 - core).wait_recv()
                mate_copy(s, ox, o, core).wait_send()
            for ox in range(1, n_x):
                forward_x(s, ox, o).wait_send()

        @pl.loop(0, n_dp)
        def _(d):
            moved = jnp.dot(perm_ref[...], gath[s, d], preferred_element_type=F32)
            gath[s, d] = moved.astype(BF16)

    def piece(s, c):
        rows = pl.ds(pl.multiple_of(c * group, 16), group)
        return jnp.concatenate([gath[s, d, rows, :] for d in range(n_dp)], axis=0)

    def put_part(s, c, value):
        rows = pl.ds(pl.multiple_of(c * group, 16), group)
        for d in range(n_dp):
            part[s, d, rows, :] = value[d * group:(d + 1) * group]

    def cols(c):
        return pl.ds(pl.multiple_of(c * chunk, 128), chunk)

    def pair_copy(s, xi):
        return pltpu.make_async_remote_copy(
            src_ref=part.at[s, 2 * xi + (1 - core)], dst_ref=pair_in.at[s, xi],
            send_sem=c_snd.at[s, xi], recv_sem=c_rcv.at[s, xi],
            device_id=(mate, ex), device_id_type=MESH,
        )

    def cross_copy(s, ox):
        return pltpu.make_async_remote_copy(
            src_ref=part.at[s, xpeer(ox)], dst_ref=cross_in.at[s, ox - 1],
            send_sem=r_snd.at[s, ox], recv_sem=r_rcv.at[s, ox],
            device_id=(xpeer(ox), ex), device_id_type=MESH,
        )

    def pair_sum(s):
        for ox in [*range(1, n_x), 0]:
            xi = (x + ox) % n_x
            pair_copy(s, xi).wait_recv()
            mine = 2 * xi + core
            total = part[s, mine].astype(F32) + pair_in[s, xi].astype(F32)
            part[s, mine] = total.astype(BF16)
            if ox:
                cross_copy(s, ox).start()

    def back_copy(s, o, to):
        dest = (ex + o) % n_ex
        return pltpu.make_async_remote_copy(
            src_ref=send.at[s, rows_of(dest)], dst_ref=back_in.at[s, rows_of(to)],
            send_sem=b_snd.at[s, o], recv_sem=b_rcv.at[s, o],
            device_id=(dp, dest), device_id_type=MESH,
        )

    def send_back(s):
        total = part[s, dp].astype(F32)
        for ox in range(1, n_x):
            cross_copy(s, ox).wait_recv()
            total = total + cross_in[s, ox - 1].astype(F32)

        @pl.loop(1, n_ex)
        def _(o):
            a2a(s, o, ex).wait_send()

        moved = jnp.dot(perm_t_ref[...], total.astype(BF16), preferred_element_type=F32)
        send[s] = moved.astype(BF16)
        back_in[s, rows_of(ex), :] = send[s, rows_of(ex), :]

        @pl.loop(1, n_ex)
        def _(o):
            back_copy(s, o, ex).start()

    def returned(s):
        @pl.loop(1, n_ex)
        def _(o):
            back_copy(s, o, (ex + n_ex - o) % n_ex).wait_recv()

    both = place[0] + place[1]
    send[0] = contract(both, stacked(tok_ref[...]), 0, 0).astype(BF16)
    pl.semaphore_wait(barrier, n_ex - 1 + n_x)
    launch(0)
    og = og_ref[...].astype(F32)
    scaled0 = stacked((og * mix_ref[:, 0:1]).astype(BF16))
    scaled1 = stacked((og * mix_ref[:, 1:2]).astype(BF16))
    send[1] = (contract(place[0], scaled0, 0, 0) + contract(place[1], scaled1, 0, 0)).astype(BF16)
    launch(1)

    spread_own(0, 0)

    @pl.loop(1, n_ex)
    def _(o):
        own_arrival(0, o)

    spread_own(1, 0)
    spread_cross(0, 0)

    @pl.loop(1, n_ex)
    def _(o):
        own_arrival(1, o)
        spread_cross(0, o)

    gathered(0)
    up_load.wait()
    pre_act[...] = jnp.zeros_like(pre_act)

    @pl.loop(0, CHUNKS)
    def _(c):
        pre_act[...] += jnp.dot(piece(0, c), up_v[cols(c), :], preferred_element_type=F32)

    act = pre_act[...]
    hidden[...] = (act * jax.nn.sigmoid(act)).astype(BF16)
    down_load.wait()

    @pl.loop(0, CHUNKS)
    def _(c):
        put_part(0, c, jnp.dot(hidden[...], down_v[:, cols(c)], preferred_element_type=F32).astype(BF16))

    for xi in range(n_x):
        pair_copy(0, xi).start()

    @pl.loop(0, n_ex)
    def _(o):
        spread_cross(1, o)

    pair_sum(0)
    gathered(1)

    act = pre_act[...]
    squash = jax.nn.sigmoid(act)
    pre_act[...] = jnp.zeros_like(pre_act)

    @pl.loop(0, CHUNKS)
    def _(c):
        pre_act[...] += contract(piece(1, c), down_v[:, cols(c)], 1, 1)

    pre_grad[...] = (pre_act[...] * (squash * (1.0 + act * (1.0 - squash)))).astype(BF16)

    @pl.loop(0, CHUNKS)
    def _(c):
        put_part(1, c, contract(pre_grad[...], up_v[cols(c), :], 1, 1).astype(BF16))

    for xi in range(n_x):
        pair_copy(1, xi).start()
    send_back(0)
    pair_sum(1)

    def up_store(c):
        return pltpu.make_async_copy(up_v.at[cols(c), :], up_out.at[cols(c), :], out_sem.at[0, c])

    def down_store(c):
        return pltpu.make_async_copy(down_v.at[:, cols(c)], down_out.at[:, cols(c)], out_sem.at[1, c])

    @pl.loop(0, CHUNKS)
    def _(c):
        up_v[cols(c), :] = contract(piece(0, c), pre_grad[...], 0, 0).astype(BF16)
        up_store(c).start()

    send_back(1)

    @pl.loop(0, CHUNKS)
    def _(c):
        down_v[:, cols(c)] = contract(hidden[...], piece(1, c), 0, 0).astype(BF16)
        down_store(c).start()

    returned(0)
    weight = (
        place[0].astype(F32) * jnp.concatenate([mix_ref[:, 0:1]] * CHUNKS, axis=0)
        + place[1].astype(F32) * jnp.concatenate([mix_ref[:, 1:2]] * CHUNKS, axis=0)
    )
    high = weight.astype(BF16)
    low = (weight - high.astype(F32)).astype(BF16)
    value = back_in[0]
    out = jnp.dot(high, value, preferred_element_type=F32) + jnp.dot(
        low, value, preferred_element_type=F32
    )
    for c in range(CHUNKS):
        lay_ref[:, c * chunk:(c + 1) * chunk] = out[c * toks:(c + 1) * toks].astype(BF16)
    returned(1)
    out = jnp.dot(place[0] + place[1], back_in[1], preferred_element_type=F32)
    for c in range(CHUNKS):
        tg_ref[:, c * chunk:(c + 1) * chunk] = out[c * toks:(c + 1) * toks].astype(BF16)

    for s in range(2):
        @pl.loop(1, n_ex)
        def _(o):
            back_copy(s, o, ex).wait_send()

        for xi in range(n_x):
            pair_copy(s, xi).wait_send()
        for ox in range(1, n_x):
            cross_copy(s, ox).wait_send()

    @pl.loop(0, CHUNKS)
    def _(c):
        up_store(c).wait()
        down_store(c).wait()


def per_device(tokens, expert_ids, mix_weights, w_up, w_down, out_grad):
    toks, width = tokens.shape
    n_dp, n_ex = lax.axis_size("dp"), lax.axis_size("expert")
    hid = w_up.shape[2]
    limit = max(2, 3 * toks // n_ex)
    cap = -(-limit // 4) * 4
    chunk = width // CHUNKS
    block = CHUNKS * cap
    slots, group = n_ex * block, n_ex * cap
    rows = n_dp * group
    n_x = n_dp // 2
    perm = np.zeros((slots, slots), np.float32)
    for c in range(CHUNKS):
        for e in range(n_ex):
            for s in range(cap):
                perm[c * group + e * cap + s, e * block + c * cap + s] = 1
    vmem = pl.BlockSpec(memory_space=pltpu.VMEM)
    hbm = pl.BlockSpec(memory_space=pl.ANY)
    dma = pltpu.SemaphoreType.DMA
    cross = max(1, n_x - 1)
    layer_out, token_grad, up_grad, down_grad = pl.pallas_call(
        functools.partial(kernel, n_dp, n_ex, cap),
        out_shape=(
            jax.ShapeDtypeStruct((toks, width), BF16),
            jax.ShapeDtypeStruct((toks, width), BF16),
            jax.ShapeDtypeStruct((width, hid), BF16),
            jax.ShapeDtypeStruct((hid, width), BF16),
        ),
        in_specs=[vmem] * 6 + [hbm] * 2,
        out_specs=(vmem, vmem, hbm, hbm),
        scratch_shapes=[
            pltpu.VMEM((2, CHUNKS * toks, slots), BF16),
            pltpu.VMEM((width, hid), BF16),
            pltpu.VMEM((hid, width), BF16),
            pltpu.VMEM((2, slots, chunk), BF16),
            pltpu.VMEM((2, n_dp, slots, chunk), BF16),
            pltpu.VMEM((2, n_dp, slots, chunk), BF16),
            pltpu.VMEM((rows, hid), F32),
            pltpu.VMEM((rows, hid), BF16),
            pltpu.VMEM((rows, hid), BF16),
            pltpu.VMEM((2, n_x, slots, chunk), BF16),
            pltpu.VMEM((2, cross, slots, chunk), BF16),
            pltpu.VMEM((2, slots, chunk), BF16),
            dma((2,)),
            dma((2, n_ex)), dma((2, n_ex)),
            dma((2, n_x, n_ex)), dma((2, n_x, n_ex)),
            dma((2, n_x, n_ex)), dma((2, n_x, n_ex)),
            dma((2, n_x)), dma((2, n_x)),
            dma((2, n_x)), dma((2, n_x)),
            dma((2, n_ex)), dma((2, n_ex)),
            dma((2, CHUNKS)),
        ],
        compiler_params=pltpu.CompilerParams(
            collective_id=0, has_side_effects=True, vmem_limit_bytes=62 * 1024 * 1024
        ),
        cost_estimate=pl.CostEstimate(
            flops=12 * rows * width * hid,
            bytes_accessed=8 * width * hid,
            transcendentals=2 * rows * hid,
        ),
    )(
        expert_ids, mix_weights, tokens, out_grad,
        jnp.asarray(perm, BF16), jnp.asarray(perm.T, BF16), w_up[0], w_down[0],
    )
    return layer_out, token_grad, up_grad[None], down_grad[None]


def solution(mesh):
    in_specs = (
        P(("dp", "expert"), None),
        P(("dp", "expert"), None),
        P(("dp", "expert"), None),
        P("expert", None, "dp"),
        P("expert", "dp", None),
        P(("dp", "expert"), None),
    )
    out_specs = (
        P(("dp", "expert"), None),
        P(("dp", "expert"), None),
        P("expert", None, "dp"),
        P("expert", "dp", None),
    )
    return jax.shard_map(
        per_device, mesh=mesh, in_specs=in_specs, out_specs=out_specs, check_vma=False
    )
```

time: 211 us -> 116 us (0.55); the launches traced: 207 us -> 116 us
  Pallas kernels: 0 us -> 101 us
  waiting for transfers between devices: 77.8 us -> 0 us
  blocking collectives: 52.5 us -> 0 us
  matrix products: 40.5 us -> 0 us
  between operations: 13.9 us -> 0.64 us
  starting transfers between devices: 12.2 us -> 0 us
  local copies, waits for them, and re-layouts: 8.75 us -> 14.1 us
    pallas_call x0 -> x1, Pallas kernels: none -> 101 us  [per_device(): pl.pallas_call(functools.partial(kernel, n_dp, n_ex, cap), out_shape=(jax...]
    reduce_scatter x2 -> x0, waiting for transfers between devices: 55.8 us -> none  [per_device(): lax.psum_scatter(lax.optimization_barrier(term.astype(jnp.bfloat16)).asty...]
    all_to_all x2 -> x0, blocking collectives: 52.5 us -> none  [the longest x1 26.4 us: spread(): lax.all_to_all(token_send, 'expert', split_axis=0, concat_axis=0, tiled=T...]
    dot_general x10 -> x0, matrix products: 40.5 us -> none  [the longest x1 7.55 us: per_device(): lax.dot_general(token_rows, pre_grad, (((0,), (0,)), ((), ())), preferred...]
    all_gather x2 -> x0, waiting for transfers between devices: 15.1 us -> none  [the longest x1 15.1 us: spread(): lax.all_gather(grad_moved, 'dp', axis=0, tiled=True)]
    unnamed x11 -> x10, local copies, waits for them, and re-layouts: 1.65 us -> 14.1 us
    all_to_all x2 -> x0, starting transfers between devices: 12 us -> none  [the longest x1 6 us: per_device(): lax.all_to_all(in_rows, 'expert', split_axis=0, concat_axis=0, tiled=True)]
    all_to_all x2 -> x0, waiting for transfers between devices: 6.87 us -> none  [the longest x1 6.87 us: per_device(): lax.all_to_all(in_rows, 'expert', split_axis=0, concat_axis=0, tiled=True)]
  transfers between devices with their start and end apart: 6 -> 0, of which waited for: 4 -> 0; matrix products, arithmetic and copies ran while one was open for 19% -> 0% of each run, Pallas kernels for 0% -> 0%
where the time goes in v1:
time: 116 us
  Pallas kernels  101 us (87%)
  local copies, waits for them, and re-layouts  14.1 us (12%)
    pallas_call x1, Pallas kernels, per_device(): pl.pallas_call(functools.partial(kernel, n_dp, n_ex, cap), out_shape=(jax...  101 us
    unnamed x10, local copies, waits for them, and re-layouts  14.1 us

profile of v1, /device:TPU:28, one launch (start us, length us, event | category | flops | bytes accessed | tf_op | source)
XLA Modules:
  0.0 116.0 jit_solution(18347855989575233417)
XLA Ops:
  0.6 1.4 %copy.12.ids_ref = s32[32,2]{1,0:T(8,128)} copy(s32[32,2]{0,1:T(2,128)} %param.9) | data formatting | bytes 512 | tf_op args[1]
  2.0 1.4 %copy.13.mix_ref = f32[32,2]{1,0:T(8,128)} copy(f32[32,2]{0,1:T(2,128)} %param.10) | data formatting | bytes 512 | tf_op args[2]
  3.4 101.2 %shard_map.111 = (bf16[32,3584]{1,0:T(8,128)(2,1)}, bf16[32,3584]{1,0:T(8,128)(2,1)}, bf16[3584,768]{1,0:T(8,128)(2,1)}, bf16[768,3584]{1,0:T(8,128)(2,1)}) custom-call(s32[32,2]{1,0:T(8,128)} %copy.12.ids_ref, f32[32,2]{1,0:T(8,128)} %copy.13.mix_ref, bf16[32,3584]{1,0:T(8,128)(2,1)} %tok_ref.1, bf16[32,3584]{1,0:T(8,128)(2,1)} %og_ref.1, ...), custom_call_target="tpu_custom_call" | custom-call | flops 12683575296 | bytes 22020096 | tf_op jit(solution)/shard_map/pallas_call | solution.py:370
  104.6 1.6 %copy.18 = bf16[32,3584]{1,0:T(8,128)(2,1)} copy(bf16[32,3584]{1,0:T(8,128)(2,1)} %get-tuple-element.16) | data formatting | bytes 458752
  106.2 0.0 slice-start
  106.3 1.8 %copy.19 = bf16[32,3584]{1,0:T(8,128)(2,1)} copy(bf16[32,3584]{1,0:T(8,128)(2,1)} %get-tuple-element.17) | data formatting | bytes 458752
  108.0 0.0 slice-start.1
  108.0 5.5 %copy.20 = bf16[1,3584,768]{2,1,0:T(8,128)(2,1)} copy(bf16[1,3584,768]{2,1,0:T(8,128)(2,1)} %bitcast.7) | data formatting | bytes 11010048
  113.5 0.0 slice-done
  113.5 0.0 slice-done.1
  113.5 2.4 %copy.21 = bf16[1,768,3584]{2,1,0:T(8,128)(2,1)} copy(bf16[1,768,3584]{2,1,0:T(8,128)(2,1)S(1)} %bitcast.6) | data formatting | bytes 11010048
  (1 shorter events, 0.0 us)
Async XLA Ops:
  106.2 7.3 %slice-start = ((s8[5505024]{0:T(1024)(128)(4,1)}), s8[4194304]{0:T(1024)(128)(4,1)S(1)}, s32[]{:S(2)}) async-start(s8[5505024]{0:T(1024)(128)(4,1)} %bitcast.4), calls=%async_computation | async-start | bytes 8388608
  108.0 5.5 %slice-start.1 = ((s8[5505024]{0:T(1024)(128)(4,1)}), s8[1310720]{0:T(1024)(128)(4,1)S(1)}, s32[]{:S(2)}) async-start(s8[5505024]{0:T(1024)(128)(4,1)} %bitcast.4), calls=%async_computation.1 | async-start | bytes 2621440

commit v2 on v1

--- a/solution.py
+++ b/solution.py
@@ -39,6 +39,8 @@
     core = dp % 2
     mate = 2 * x + (1 - core)
 
+    bits = [1 << i for i in range(n_ex.bit_length() - 1)]
+
     def xpeer(o):
         return 2 * ((x + o) % n_x) + core
 
@@ -57,29 +59,46 @@
     up_load.start()
     down_load.start()
 
-    lower = (
-        lax.broadcasted_iota(jnp.int32, (toks, toks), 1)
-        < lax.broadcasted_iota(jnp.int32, (toks, toks), 0)
-    )
-    lower = jnp.where(lower, 1.0, 0.0).astype(BF16)
-    lane = lax.broadcasted_iota(jnp.int32, (toks, n_ex), 1)
-    id0, id1 = ids_ref[:, 0:1], ids_ref[:, 1:2]
-    hit0 = jnp.where(lane == id0, 1.0, 0.0)
-    hit1 = jnp.where(lane == id1, 1.0, 0.0)
-    before0 = jnp.dot(lower, hit0.astype(BF16), preferred_element_type=F32)
-    before1 = jnp.dot(lower, hit1.astype(BF16), preferred_element_type=F32) + jnp.sum(
-        hit0, axis=0, keepdims=True
-    )
-    pos0 = jnp.sum(before0 * hit0, axis=1, keepdims=True).astype(jnp.int32)
-    pos1 = jnp.sum(before1 * hit1, axis=1, keepdims=True).astype(jnp.int32)
-    slot = lax.broadcasted_iota(jnp.int32, (toks, slots), 1)
-    for k, (ids, pos) in enumerate(((id0, pos0), (id1, pos1))):
-        for c in range(CHUNKS):
-            hit = slot == ids * block + pos + c * cap
-            place[k, c * toks:(c + 1) * toks, :] = jnp.where(hit, 1.0, 0.0).astype(BF16)
+    wide = CHUNKS * toks
+
+    def iota(shape, dim):
+        return lax.broadcasted_iota(jnp.int32, shape, dim)
+
+    def ones(where):
+        return jnp.where(where, 1.0, 0.0)
+
+    earlier = ones(iota((toks, toks), 0) < iota((toks, toks), 1)).astype(BF16)
+    tile = sum(
+        ones(iota((toks, wide), 1) == iota((toks, wide), 0) + c * toks) for c in range(CHUNKS)
+    ).astype(BF16)
+
+    def tiled(row):
+        full = jnp.broadcast_to(row, (8, toks)).astype(BF16)
+        return jnp.dot(full, tile, preferred_element_type=F32)[0:1]
+
+    hits = [ones(iota((n_ex, toks), 0) == ids_ref[k:k + 1, :]) for k in range(2)]
+    before = [jnp.dot(hit.astype(BF16), earlier, preferred_element_type=F32) for hit in hits]
+    before[1] = before[1] + jnp.sum(hits[0], axis=1, keepdims=True)
+    ids = ids_ref[...]
+    rank_ids = ((ids >> 1) & 1) * (n_ex // 2) + (ids >> 2) * 2 + (ids & 1)
+    lane_chunk = sum(jnp.where(iota((1, wide), 1) >= c * toks, 1, 0) for c in range(1, CHUNKS))
+    for k in range(2):
+        pos = jnp.sum(before[k] * hits[k], axis=0, keepdims=True)
+        target = tiled(rank_ids[k:k + 1, :].astype(F32)) * block + tiled(pos)
+        target = target.astype(jnp.int32) + lane_chunk * cap
+        place[k] = ones(iota((slots, wide), 0) == target).astype(BF16)
+
+    def rank(e):
+        return (e // 2) % 2 * (n_ex // 2) + e // 4 * 2 + e % 2
 
     def rows_of(e):
-        return pl.ds(pl.multiple_of(e * block, 16), block)
+        return pl.ds(pl.multiple_of(rank(e) * block, 16), block)
+
+    def half_rows(h):
+        return pl.ds(h * (slots // 2), slots // 2)
+
+    def swap(o):
+        return sum((ex // bit + o // bit) % 2 * bit for bit in bits)
 
     def stacked(value):
         return jnp.concatenate(
@@ -87,7 +106,7 @@
         )
 
     def a2a(s, o, to):
-        src = (ex + o) % n_ex
+        src = swap(o)
         return pltpu.make_async_remote_copy(
             src_ref=send.at[s, rows_of(src)],
             dst_ref=gath.at[s, dp, rows_of(to)],
@@ -96,7 +115,7 @@
         )
 
     def forward_x(s, ox, o):
-        src = (ex + n_ex - o) % n_ex
+        src = swap(o)
         return pltpu.make_async_remote_copy(
             src_ref=gath.at[s, dp, rows_of(src)],
             dst_ref=gath.at[s, dp, rows_of(src)],
@@ -105,7 +124,7 @@
         )
 
     def arrived_x(s, ox, o):
-        src = (ex + n_ex - o) % n_ex
+        src = swap(o)
         owner = 2 * xsource(ox) + core
         return pltpu.make_async_remote_copy(
             src_ref=gath.at[s, owner, rows_of(src)],
@@ -115,7 +134,7 @@
         )
 
     def mate_copy(s, ox, o, half):
-        src = (ex + n_ex - o) % n_ex
+        src = swap(o)
         owner = 2 * xsource(ox) + half
         return pltpu.make_async_remote_copy(
             src_ref=gath.at[s, owner, rows_of(src)],
@@ -124,12 +143,8 @@
             device_id=(mate, ex), device_id_type=MESH,
         )
 
-    def launch(s):
+    def keep_own(s):
         gath[s, dp, rows_of(ex), :] = send[s, rows_of(ex), :]
-
-        @pl.loop(1, n_ex)
-        def _(o):
-            a2a(s, o, ex).start()
 
     def spread_own(s, o):
         for ox in range(1, n_x):
@@ -142,7 +157,7 @@
             mate_copy(s, ox, o, core).start()
 
     def own_arrival(s, o):
-        a2a(s, o, (ex + n_ex - o) % n_ex).wait_recv()
+        a2a(s, o, swap(o)).wait_recv()
         spread_own(s, o)
 
     def gathered(s):
@@ -156,17 +171,27 @@
 
         @pl.loop(0, n_dp)
         def _(d):
-            moved = jnp.dot(perm_ref[...], gath[s, d], preferred_element_type=F32)
-            gath[s, d] = moved.astype(BF16)
+            for h in range(2):
+                moved = jnp.dot(perm_ref[...], gath[s, d, half_rows(h), :], preferred_element_type=F32)
+                gath[s, d, half_rows(h), :] = moved.astype(BF16)
+
+    def strips(c):
+        return [
+            pl.ds(pl.multiple_of(h * (slots // 2) + c * (group // 2), 16), group // 2)
+            for h in range(2)
+        ]
 
     def piece(s, c):
-        rows = pl.ds(pl.multiple_of(c * group, 16), group)
-        return jnp.concatenate([gath[s, d, rows, :] for d in range(n_dp)], axis=0)
+        return jnp.concatenate(
+            [gath[s, d, rows, :] for d in range(n_dp) for rows in strips(c)], axis=0
+        )
 
     def put_part(s, c, value):
-        rows = pl.ds(pl.multiple_of(c * group, 16), group)
+        size = group // 2
         for d in range(n_dp):
-            part[s, d, rows, :] = value[d * group:(d + 1) * group]
+            for h, rows in enumerate(strips(c)):
+                at = (2 * d + h) * size
+                part[s, d, rows, :] = value[at:at + size]
 
     def cols(c):
         return pl.ds(pl.multiple_of(c * chunk, 128), chunk)
@@ -178,10 +203,11 @@
             device_id=(mate, ex), device_id_type=MESH,
         )
 
-    def cross_copy(s, ox):
-        return pltpu.make_async_remote_copy(
-            src_ref=part.at[s, xpeer(ox)], dst_ref=cross_in.at[s, ox - 1],
-            send_sem=r_snd.at[s, ox], recv_sem=r_rcv.at[s, ox],
+    def cross_copy(s, ox, h):
+        return pltpu.make_async_remote_copy(
+            src_ref=part.at[s, xpeer(ox), half_rows(h)],
+            dst_ref=cross_in.at[s, ox - 1, half_rows(h)],
+            send_sem=r_snd.at[s, ox, h], recv_sem=r_rcv.at[s, ox, h],
             device_id=(xpeer(ox), ex), device_id_type=MESH,
         )
 
@@ -190,57 +216,77 @@
             xi = (x + ox) % n_x
             pair_copy(s, xi).wait_recv()
             mine = 2 * xi + core
-            total = part[s, mine].astype(F32) + pair_in[s, xi].astype(F32)
-            part[s, mine] = total.astype(BF16)
-            if ox:
-                cross_copy(s, ox).start()
-
-    def back_copy(s, o, to):
-        dest = (ex + o) % n_ex
-        return pltpu.make_async_remote_copy(
-            src_ref=send.at[s, rows_of(dest)], dst_ref=back_in.at[s, rows_of(to)],
-            send_sem=b_snd.at[s, o], recv_sem=b_rcv.at[s, o],
+            for h in range(2):
+                rows = half_rows(h)
+                total = part[s, mine, rows, :].astype(F32) + pair_in[s, xi, rows, :].astype(F32)
+                part[s, mine, rows, :] = total.astype(BF16)
+                if ox:
+                    cross_copy(s, ox, h).start()
+
+    def back_copy(s, source, dest):
+        return pltpu.make_async_remote_copy(
+            src_ref=send.at[s, rows_of(dest)], dst_ref=back_in.at[s, rows_of(source)],
+            send_sem=b_snd.at[s, dest], recv_sem=b_rcv.at[s, source],
             device_id=(dp, dest), device_id_type=MESH,
         )
 
-    def send_back(s):
-        total = part[s, dp].astype(F32)
-        for ox in range(1, n_x):
-            cross_copy(s, ox).wait_recv()
-            total = total + cross_in[s, ox - 1].astype(F32)
-
+    def sent(s):
         @pl.loop(1, n_ex)
         def _(o):
             a2a(s, o, ex).wait_send()
 
+    def send_back(s, h):
+        rows = half_rows(h)
+        total = part[s, dp, rows, :].astype(F32)
+        for ox in range(1, n_x):
+            cross_copy(s, ox, h).wait_recv()
+            total = total + cross_in[s, ox - 1, rows, :].astype(F32)
         moved = jnp.dot(perm_t_ref[...], total.astype(BF16), preferred_element_type=F32)
-        send[s] = moved.astype(BF16)
-        back_in[s, rows_of(ex), :] = send[s, rows_of(ex), :]
-
-        @pl.loop(1, n_ex)
+        send[s, rows, :] = moved.astype(BF16)
+
+        @pl.loop(0, n_ex)
         def _(o):
-            back_copy(s, o, ex).start()
+            dest = swap(o)
+
+            @pl.when(dest // 2 % 2 == h)
+            def _():
+                @pl.when(o > 0)
+                def _():
+                    back_copy(s, ex, dest).start()
+
+                @pl.when(o == 0)
+                def _():
+                    back_in[s, rows_of(ex), :] = send[s, rows_of(ex), :]
 
     def returned(s):
         @pl.loop(1, n_ex)
         def _(o):
-            back_copy(s, o, (ex + n_ex - o) % n_ex).wait_recv()
+            back_copy(s, swap(o), swap(o)).wait_recv()
 
     both = place[0] + place[1]
-    send[0] = contract(both, stacked(tok_ref[...]), 0, 0).astype(BF16)
+    send[0] = jnp.dot(both, stacked(tok_ref[...]), preferred_element_type=F32).astype(BF16)
     pl.semaphore_wait(barrier, n_ex - 1 + n_x)
-    launch(0)
+    keep_own(0)
+
+    @pl.loop(1, n_ex)
+    def _(o):
+        a2a(0, o, ex).start()
+
+    spread_own(0, 0)
     og = og_ref[...].astype(F32)
-    scaled0 = stacked((og * mix_ref[:, 0:1]).astype(BF16))
-    scaled1 = stacked((og * mix_ref[:, 1:2]).astype(BF16))
-    send[1] = (contract(place[0], scaled0, 0, 0) + contract(place[1], scaled1, 0, 0)).astype(BF16)
-    launch(1)
-
-    spread_own(0, 0)
+    eye = iota((toks, toks), 0) == iota((toks, toks), 1)
+    mixed = []
+    for k in range(2):
+        column = jnp.sum(jnp.where(eye, mix_ref[k:k + 1, :], 0.0), axis=1, keepdims=True)
+        scaled = stacked((og * column).astype(BF16))
+        mixed.append(jnp.dot(place[k], scaled, preferred_element_type=F32))
+    send[1] = (mixed[0] + mixed[1]).astype(BF16)
+    keep_own(1)
 
     @pl.loop(1, n_ex)
     def _(o):
         own_arrival(0, o)
+        a2a(1, o, ex).start()
 
     spread_own(1, 0)
     spread_cross(0, 0)
@@ -292,7 +338,9 @@
 
     for xi in range(n_x):
         pair_copy(1, xi).start()
-    send_back(0)
+    sent(0)
+    send_back(0, 0)
+    send_back(0, 1)
     pair_sum(1)
 
     def up_store(c):
@@ -306,40 +354,41 @@
         up_v[cols(c), :] = contract(piece(0, c), pre_grad[...], 0, 0).astype(BF16)
         up_store(c).start()
 
-    send_back(1)
+    sent(1)
+    send_back(1, 0)
 
     @pl.loop(0, CHUNKS)
     def _(c):
         down_v[:, cols(c)] = contract(hidden[...], piece(1, c), 0, 0).astype(BF16)
         down_store(c).start()
 
+    send_back(1, 1)
     returned(0)
-    weight = (
-        place[0].astype(F32) * jnp.concatenate([mix_ref[:, 0:1]] * CHUNKS, axis=0)
-        + place[1].astype(F32) * jnp.concatenate([mix_ref[:, 1:2]] * CHUNKS, axis=0)
-    )
-    high = weight.astype(BF16)
-    low = (weight - high.astype(F32)).astype(BF16)
+    high = low = 0.0
+    for k in range(2):
+        row = mix_ref[k:k + 1, :]
+        upper = row.astype(BF16).astype(F32)
+        high = high + place[k].astype(F32) * tiled(upper)
+        low = low + place[k].astype(F32) * tiled(row - upper)
     value = back_in[0]
-    out = jnp.dot(high, value, preferred_element_type=F32) + jnp.dot(
-        low, value, preferred_element_type=F32
-    )
+    out = contract(high.astype(BF16), value, 0, 0) + contract(low.astype(BF16), value, 0, 0)
     for c in range(CHUNKS):
         lay_ref[:, c * chunk:(c + 1) * chunk] = out[c * toks:(c + 1) * toks].astype(BF16)
     returned(1)
-    out = jnp.dot(place[0] + place[1], back_in[1], preferred_element_type=F32)
+    out = contract(place[0] + place[1], back_in[1], 0, 0)
     for c in range(CHUNKS):
         tg_ref[:, c * chunk:(c + 1) * chunk] = out[c * toks:(c + 1) * toks].astype(BF16)
 
     for s in range(2):
         @pl.loop(1, n_ex)
         def _(o):
-            back_copy(s, o, ex).wait_send()
+            back_copy(s, ex, swap(o)).wait_send()
 
         for xi in range(n_x):
             pair_copy(s, xi).wait_send()
         for ox in range(1, n_x):
-            cross_copy(s, ox).wait_send()
+            for h in range(2):
+                cross_copy(s, ox, h).wait_send()
 
     @pl.loop(0, CHUNKS)
     def _(c):
@@ -358,11 +407,12 @@
     slots, group = n_ex * block, n_ex * cap
     rows = n_dp * group
     n_x = n_dp // 2
-    perm = np.zeros((slots, slots), np.float32)
+    part = n_ex // 2
+    perm = np.zeros((slots // 2, slots // 2), np.float32)
     for c in range(CHUNKS):
-        for e in range(n_ex):
+        for e in range(part):
             for s in range(cap):
-                perm[c * group + e * cap + s, e * block + c * cap + s] = 1
+                perm[c * part * cap + e * cap + s, e * block + c * cap + s] = 1
     vmem = pl.BlockSpec(memory_space=pltpu.VMEM)
     hbm = pl.BlockSpec(memory_space=pl.ANY)
     dma = pltpu.SemaphoreType.DMA
@@ -378,7 +428,7 @@
         in_specs=[vmem] * 6 + [hbm] * 2,
         out_specs=(vmem, vmem, hbm, hbm),
         scratch_shapes=[
-            pltpu.VMEM((2, CHUNKS * toks, slots), BF16),
+            pltpu.VMEM((2, slots, CHUNKS * toks), BF16),
             pltpu.VMEM((width, hid), BF16),
             pltpu.VMEM((hid, width), BF16),
             pltpu.VMEM((2, slots, chunk), BF16),
@@ -395,7 +445,7 @@
             dma((2, n_x, n_ex)), dma((2, n_x, n_ex)),
             dma((2, n_x, n_ex)), dma((2, n_x, n_ex)),
             dma((2, n_x)), dma((2, n_x)),
-            dma((2, n_x)), dma((2, n_x)),
+            dma((2, n_x, 2)), dma((2, n_x, 2)),
             dma((2, n_ex)), dma((2, n_ex)),
             dma((2, CHUNKS)),
         ],
@@ -408,7 +458,7 @@
             transcendentals=2 * rows * hid,
         ),
     )(
-        expert_ids, mix_weights, tokens, out_grad,
+        expert_ids.T, mix_weights.T, tokens, out_grad,
         jnp.asarray(perm, BF16), jnp.asarray(perm.T, BF16), w_up[0], w_down[0],
     )
     return layer_out, token_grad, up_grad[None], down_grad[None]

time: 116 us -> 109 us (0.940)
  Pallas kernels: 101 us -> 96.2 us
  local copies, waits for them, and re-layouts: 14.1 us -> 11.3 us
    pallas_call x1, Pallas kernels: 101 us -> 96.2 us  [per_device(): pl.pallas_call(functools.partial(kernel, n_dp, n_ex, cap), out_shape=(jax...]
    unnamed x10 -> x8, local copies, waits for them, and re-layouts: 14.1 us -> 11.3 us
where the time goes in v2:
time: 109 us; the launch traced here: 108 us
  Pallas kernels  96.2 us (88%)
  local copies, waits for them, and re-layouts  11.3 us (10%)
    pallas_call x1, Pallas kernels, per_device(): pl.pallas_call(functools.partial(kernel, n_dp, n_ex, cap), out_shape=(jax...  96.2 us
    unnamed x8, local copies, waits for them, and re-layouts  11.3 us

profile of v2, /device:TPU:28, one launch (start us, length us, event | category | flops | bytes accessed | tf_op | source)
XLA Modules:
  0.0 108.2 jit_solution(1195085356086285468)
XLA Ops:
  0.6 96.2 %shard_map.111 = (bf16[32,3584]{1,0:T(8,128)(2,1)}, bf16[32,3584]{1,0:T(8,128)(2,1)}, bf16[3584,768]{1,0:T(8,128)(2,1)}, bf16[768,3584]{1,0:T(8,128)(2,1)}) custom-call(s32[2,32]{1,0:T(2,128)} %bitcast.12, f32[2,32]{1,0:T(2,128)} %bitcast.13, bf16[32,3584]{1,0:T(8,128)(2,1)} %tok_ref.1, bf16[32,3584]{1,0:T(8,128)(2,1)} %og_ref.1, ...), custom_call_target="tpu_custom_call" | custom-call | flops 12683575296 | bytes 22020096 | tf_op jit(solution)/shard_map/pallas_call | solution.py:420
  96.9 1.6 %copy.16 = bf16[32,3584]{1,0:T(8,128)(2,1)} copy(bf16[32,3584]{1,0:T(8,128)(2,1)} %get-tuple-element.16) | data formatting | bytes 458752
  98.5 0.0 slice-start
  98.5 1.8 %copy.17 = bf16[32,3584]{1,0:T(8,128)(2,1)} copy(bf16[32,3584]{1,0:T(8,128)(2,1)} %get-tuple-element.17) | data formatting | bytes 458752
  100.3 0.0 slice-start.1
  100.3 5.5 %copy.18 = bf16[1,3584,768]{2,1,0:T(8,128)(2,1)} copy(bf16[1,3584,768]{2,1,0:T(8,128)(2,1)} %bitcast.9) | data formatting | bytes 11010048
  105.8 0.0 slice-done
  105.8 0.0 slice-done.1
  105.8 2.4 %copy.19 = bf16[1,768,3584]{2,1,0:T(8,128)(2,1)} copy(bf16[1,768,3584]{2,1,0:T(8,128)(2,1)S(1)} %bitcast.8) | data formatting | bytes 11010048
  (1 shorter events, 0.0 us)
Async XLA Ops:
  98.5 7.3 %slice-start = ((s8[5505024]{0:T(1024)(128)(4,1)}), s8[4194304]{0:T(1024)(128)(4,1)S(1)}, s32[]{:S(2)}) async-start(s8[5505024]{0:T(1024)(128)(4,1)} %bitcast.6), calls=%async_computation | async-start | bytes 8388608
  100.3 5.5 %slice-start.1 = ((s8[5505024]{0:T(1024)(128)(4,1)}), s8[1310720]{0:T(1024)(128)(4,1)S(1)}, s32[]{:S(2)}) async-start(s8[5505024]{0:T(1024)(128)(4,1)} %bitcast.6), calls=%async_computation.1 | async-start | bytes 2621440
